TPU v7x, 1024 devices: a whole 8x8x8 slice. The times are simulated.
1024 devices in a mesh: fsdp: 64 (over y, z_hi, core), head: 16 (over x, z_lo).
Axes of the slice: x: 8, y: 8, z: 8 (z_hi: 4, z_lo: 2; z = z_hi * 2 + z_lo), core: 2. Of those that a mesh axis runs over, the one named last changes fastest.
Arguments:
- query_up: bfloat16 [2, 1536, 128, 128], P(None, 'fsdp'), may hold values from -6 to 6
- key_up: bfloat16 [2, 512, 128, 128], P(None, 'head', 'fsdp'), may hold values from -0.5 to 0.5
Outputs:
- absorbed: bfloat16 [2, 128, 1536, 512], P(None, 'head', 'fsdp')
All inputs are finite; a program needn't handle non-finite values.
Results may differ from a plain program's by a relative error of at most 0.001.
Values may be sent and summed in bfloat16 or wider, within the bound.
No kernel may reach another device: no remote copies, remote signals or barrier semaphores. Data moves between devices by JAX's collectives and lax.ppermute only.
A program may use at most 32 MiB of HBM per device.

v0:
```python
import jax
import jax.numpy as jnp
from jax import lax
from jax.sharding import PartitionSpec as P


def absorb(queries, keys):
    product = jnp.einsum("lrhn,lchn->lhrc", queries, keys, preferred_element_type=jnp.float32)
    return product.astype(jnp.bfloat16)


def shards(query_up, key_up):
    gathered = lax.all_gather(key_up, "fsdp", axis=2, tiled=True)
    owned_keys = lax.all_to_all(gathered, "head", split_axis=2, concat_axis=1, tiled=True)
    head_count = owned_keys.shape[2]
    offset = lax.axis_index("head") * head_count
    own_queries = lax.dynamic_slice_in_dim(query_up, offset, head_count, 2)
    return absorb(own_queries, owned_keys)


def solution(mesh):
    return jax.shard_map(
        shards,
        mesh=mesh,
        in_specs=(P(None, "fsdp", None, None), P(None, "head", "fsdp", None)),
        out_specs=P(None, "head", "fsdp", None),
        check_vma=False,
    )
```

profile of v0, /device:TPU:32, one launch (start us, length us, event | category | flops | bytes accessed | tf_op | source)
XLA Modules:
  0.0 183.8 jit_solution(15165587273753078221)
XLA Ops:
  6.5 0.0 copy-start
  6.5 0.0 all-gather.2.cloned.1.call-start
  6.5 1.5 copy.6
  8.0 0.0 all-gather.2.cloned.1.call-update
  8.1 107.3 %all-gather.2.cloned.1.call-done = bf16[2,32,128,128]{3,1,0,2:T(8,128)(2,1)} async-done(((bf16[2,32,2,128]{3,1,0,2:T(8,128)(2,1)}), bf16[2,32,128,128]{3,1,0,2:T(8,128)(2,1)}) %all-gather.2.cloned.1.call-update) | async-done | bytes 2097168 | tf_op jit(solution)/shard_map/all_gather | solution.py:13
  115.3 6.8 %all-to-all-start = ((bf16[2,32,128,128]{3,1,0,2:T(8,128)(2,1)}), bf16[2,32,128,128]{3,1,0,2:T(8,128)(2,1)}, u32[]{:S(2)}, u32[]{:S(2)}) async-start(bf16[2,32,128,128]{3,1,0,2:T(8,128)(2,1)} %all-gather.2.cloned.1.call-done), calls=%async_computation | async-start | bytes 4194304 | tf_op jit(solution)/shard_map/all_to_all | solution.py:14
  122.1 0.0 copy-done
  122.2 50.6 %all-to-all-done = bf16[2,32,128,128]{3,1,0,2:T(8,128)(2,1)} async-done(((bf16[2,32,128,128]{3,1,0,2:T(8,128)(2,1)}), bf16[2,32,128,128]{3,1,0,2:T(8,128)(2,1)}, u32[]{:S(2)}, u32[]{:S(2)}) %all-to-all-start) | async-done | bytes 2097184 | tf_op jit(solution)/shard_map/all_to_all | solution.py:14
  172.8 2.1 %copy.7 = bf16[2,32,16,8,128]{4,1,2,3,0:T(8,128)(2,1)S(1)} copy(bf16[2,32,16,8,128]{4,1,0,3,2:T(8,128)(2,1)} %bitcast) | data formatting | bytes 4194304 | tf_op jit(solution)/shard_map/all_to_all | solution.py:14
  175.0 2.0 %convolution_convert_fusion = bf16[2,8,24,512]{3,2,1,0:T(8,128)(2,1)} fusion(bf16[2,512,8,128]{3,1,2,0:T(8,128)(2,1)S(1)} %bitcast.5, bf16[2,24,8,128]{3,2,1,0:T(8,128)(2,1)S(1)} %constant_dynamic-slice_fusion), kind=kOutput, calls=%fused_computation | convolution fusion | flops 50528256 | bytes 2588672 | tf_op jit(solution)/shard_map/lrhn,lchn->lhrc/dot_general | solution.py:8
  (1 shorter events, 0.0 us)
Async XLA Ops:
  6.5 115.6 %copy-start = (bf16[2,24,128,128]{3,2,1,0:T(8,128)(2,1)S(1)}, bf16[2,24,128,128]{3,2,1,0:T(8,128)(2,1)}, u32[]{:S(2)}) copy-start(bf16[2,24,128,128]{3,2,1,0:T(8,128)(2,1)} %param.2) | copy-start | bytes 4718596
  6.5 108.8 %all-gather.2.cloned.1.call-start = ((), (), s32[]{:S(2)}) async-start(), calls=%async_computation.1 | async-start | bytes 2129920 | tf_op jit(solution)/shard_map/all_gather | solution.py:13
  115.3 57.5 %all-to-all-start = ((bf16[2,32,128,128]{3,1,0,2:T(8,128)(2,1)}), bf16[2,32,128,128]{3,1,0,2:T(8,128)(2,1)}, u32[]{:S(2)}, u32[]{:S(2)}) async-start(bf16[2,32,128,128]{3,1,0,2:T(8,128)(2,1)} %all-gather.2.cloned.1.call-done), calls=%async_computation | async-start | bytes 4194304 | tf_op jit(solution)/shard_map/all_to_all | solution.py:14
Sparse Core Ops, SparseCore 0:
  11.8 103.4 all-gather.1
where the time goes:
time: 184 us
  waiting for transfers between devices  158 us (86%)
  between operations  13.4 us (7%)
  starting transfers between devices  6.83 us (4%)
  local copies, waits for them, and re-layouts  3.66 us (2%)
  matrix products  1.96 us (1%)
    all_gather x1, waiting for transfers between devices, shards(): gathered = lax.all_gather(key_up, 'fsdp', axis=2, tiled=True)  107 us
    all_to_all x1, waiting for transfers between devices, shards(): lax.all_to_all(gathered, 'head', split_axis=2, concat_axis=1, tiled=True)  50.6 us
    all_to_all x1, starting transfers between devices, shards(): lax.all_to_all(gathered, 'head', split_axis=2, concat_axis=1, tiled=True)  6.82 us
  transfers between devices with their start and end apart: 2, of which 2 were waited for; matrix products, arithmetic and copies ran while one was open for 0% of the time, Pallas kernels for 0%

commit v1 on v0

v1 whole, which is shorter than its diff:
```python
import itertools

import jax
import jax.numpy as jnp
from jax import lax
from jax.sharding import Mesh, PartitionSpec as P

AXES = ("yh", "yl", "zh", "core", "x", "zl")
SIZES = (4, 2, 4, 2, 8, 2)
QUERY = ("yh", "yl", "zh", "core")
HEAD = ("x", "zl")
PEERS = ("core", "yh", "yl")
BLOCKS = ("yl", "zh", "core")


def to_owner():
    index = {c: i for i, c in enumerate(itertools.product(*[range(s) for s in SIZES]))}
    pairs = []
    for (yh, yl, zh, core, x, zl), i in index.items():
        target = ((zh % 2) * 2 + core, x // 4, x % 4, zl, yh * 2 + yl, zh // 2)
        pairs.append((i, index[target]))
    return pairs


def shards(query_up, key_up):
    layers, rows, _, width = query_up.shape
    latent, pair = key_up.shape[1:3]

    held = lax.ppermute(key_up, AXES, to_owner())
    pieces = held.transpose(2, 0, 1, 3)
    pieces = jnp.broadcast_to(pieces[:, None], (pair, 4) + pieces.shape[1:])
    pieces = pieces.reshape(16, latent, width)
    keys = lax.all_to_all(pieces, BLOCKS, 0, 0, tiled=True).reshape(16 * latent, width)

    offset = lax.axis_index(HEAD) * 8
    own = lax.dynamic_slice_in_dim(query_up, offset, 8, 2)
    own = own.transpose(0, 2, 1, 3).reshape(16, rows, width)
    queries = lax.all_to_all(own, PEERS, 0, 0, tiled=True).reshape(16 * rows, width)

    product = lax.dot_general(queries, keys, (((1,), (1,)), ((), ())), preferred_element_type=jnp.float32)
    product = product.astype(jnp.bfloat16).reshape(16, rows, 16 * latent)
    out = lax.all_to_all(product, PEERS, 0, 0, tiled=True)
    return out.reshape(layers, 8, rows, 16 * latent)


def solution(mesh):
    fine = Mesh(mesh.devices.reshape(SIZES), AXES)
    return jax.shard_map(
        shards,
        mesh=fine,
        in_specs=(P(None, QUERY, None, None), P(None, HEAD, QUERY, None)),
        out_specs=P(None, HEAD, QUERY, None),
        check_vma=False,
    )
```

time: 184 us -> 74.3 us (0.40)
  the two profiles are of different devices: /device:TPU:32 before, /device:TPU:18 now
where the time goes in v1:
time: 74.3 us; the launch traced here: 73.9 us
  blocking collectives  53.5 us (72%)
  starting transfers between devices  15.3 us (21%)
  local copies, waits for them, and re-layouts  2.86 us (4%)
  waiting for transfers between devices  1.89 us (3%)
    all_to_all x1, blocking collectives, shards(): lax.all_to_all(pieces, BLOCKS, 0, 0, tiled=True).reshape(16 * latent, width)  28.3 us
    all_to_all x1, blocking collectives, shards(): out = lax.all_to_all(product, PEERS, 0, 0, tiled=True)  25.2 us
    all_to_all x1, starting transfers between devices, shards(): lax.all_to_all(own, PEERS, 0, 0, tiled=True).reshape(16 * rows, width)  7.9 us
    ppermute x1, starting transfers between devices, shards(): held = lax.ppermute(key_up, AXES, to_owner())  7.45 us
    unnamed x4, local copies, waits for them, and re-layouts  2.81 us
    ppermute x1, waiting for transfers between devices, shards(): held = lax.ppermute(key_up, AXES, to_owner())  1.89 us
  transfers between devices with their start and end apart: 2, of which 1 were waited for; matrix products, arithmetic and copies ran while one was open for 0% of the time, Pallas kernels for 0%

profile of v1, /device:TPU:18, one launch (start us, length us, event | category | flops | bytes accessed | tf_op | source)
XLA Modules:
  0.0 73.9 jit_solution(5365173909855871833)
XLA Ops:
  0.0 0.0 copy-start
  0.0 1.4 %copy-done = bf16[2,24,128,128]{3,2,1,0:T(8,128)(2,1)S(1)} copy-done((bf16[2,24,128,128]{3,2,1,0:T(8,128)(2,1)S(1)}, bf16[2,24,128,128]{3,2,1,0:T(8,128)(2,1)}, u32[]{:S(2)}) %copy-start) | copy-done | bytes 1572888
  1.4 0.7 copy.6
  2.1 7.9 %all-to-all-start = ((bf16[16,24,128]{2,1,0:T(8,128)(2,1)}), bf16[16,24,128]{2,1,0:T(8,128)(2,1)S(1)}, u32[]{:S(2)}, u32[]{:S(2)}) async-start(bf16[16,24,128]{2,1,0:T(8,128)(2,1)} %bitcast.1), calls=%async_computation | async-start | bytes 196608 | tf_op jit(solution)/shard_map/all_to_all | solution.py:38
  10.0 7.4 %collective-permute-start = (bf16[2,32,2,128]{3,2,1,0:T(2,128)(2,1)}, bf16[2,32,2,128]{3,2,1,0:T(2,128)(2,1)S(1)}, u32[]{:S(2)}, u32[]{:S(2)}) collective-permute-start(bf16[2,32,2,128]{3,2,1,0:T(2,128)(2,1)} %param.3), channel_id=1, source_target_pairs={{0,0},{1,16},{2,32},{3,48},{4,64},{5,80},{6,96},{7,112},{8,128},{9... | collective-permute-start | bytes 98312 | tf_op jit(solution)/shard_map/ppermute | solution.py:29
  17.5 1.9 %collective-permute-done = bf16[2,32,2,128]{3,2,1,0:T(2,128)(2,1)S(1)} collective-permute-done((bf16[2,32,2,128]{3,2,1,0:T(2,128)(2,1)}, bf16[2,32,2,128]{3,2,1,0:T(2,128)(2,1)S(1)}, u32[]{:S(2)}, u32[]{:S(2)}) %collective-permute-start) | collective-permute-done | bytes 32800 | tf_op jit(solution)/shard_map/ppermute | solution.py:29
  19.4 0.0 all-to-all-done
  19.4 28.3 %all_to_all.15 = bf16[16,32,128]{2,1,0:T(8,128)(2,1)S(1)} all-to-all(bf16[16,32,128]{2,1,0:T(8,128)(2,1)S(1)} %bitcast.14), channel_id=1, replica_groups=mesh['yh'=4,'yl'=2,'zh'=4,'core'=2,'x'=8,'zl'=2] {'yl','zh','core'}, dimensions={0} | all-to-all | bytes 262144 | tf_op jit(solution)/shard_map/all_to_all | solution.py:33
  47.7 0.3 convolution_convert_fusion
  47.9 25.2 %all_to_all.16 = bf16[16,24,512]{2,1,0:T(8,128)(2,1)S(1)} all-to-all(bf16[16,24,512]{2,1,0:T(8,128)(2,1)S(1)} %bitcast.11), channel_id=1, replica_groups=mesh['yh'=4,'yl'=2,'zh'=4,'core'=2,'x'=8,'zl'=2] {'core','yh','yl'}, dimensions={0} | all-to-all | bytes 786432 | tf_op jit(solution)/shard_map/all_to_all | solution.py:42
  73.2 0.7 %copy.8 = bf16[2,8,24,512]{3,2,1,0:T(8,128)(2,1)} copy(bf16[2,8,24,512]{3,2,1,0:T(8,128)(2,1)S(1)} %bitcast.12) | data formatting | bytes 786432
  (3 shorter events, 0.1 us)
Async XLA Ops:
  0.0 1.4 %copy-start = (bf16[2,24,128,128]{3,2,1,0:T(8,128)(2,1)S(1)}, bf16[2,24,128,128]{3,2,1,0:T(8,128)(2,1)}, u32[]{:S(2)}) copy-start(bf16[2,24,128,128]{3,2,1,0:T(8,128)(2,1)} %param.2) | copy-start | bytes 4718596
  2.1 17.3 %all-to-all-start = ((bf16[16,24,128]{2,1,0:T(8,128)(2,1)}), bf16[16,24,128]{2,1,0:T(8,128)(2,1)S(1)}, u32[]{:S(2)}, u32[]{:S(2)}) async-start(bf16[16,24,128]{2,1,0:T(8,128)(2,1)} %bitcast.1), calls=%async_computation | async-start | bytes 196608 | tf_op jit(solution)/shard_map/all_to_all | solution.py:38
  10.0 9.3 %collective-permute-start = (bf16[2,32,2,128]{3,2,1,0:T(2,128)(2,1)}, bf16[2,32,2,128]{3,2,1,0:T(2,128)(2,1)S(1)}, u32[]{:S(2)}, u32[]{:S(2)}) collective-permute-start(bf16[2,32,2,128]{3,2,1,0:T(2,128)(2,1)} %param.3), channel_id=1, source_target_pairs={{0,0},{1,16},{2,32},{3,48},{4,64},{5,80},{6,96},{7,112},{8,128},{9... | collective-permute-start | bytes 98312 | tf_op jit(solution)/shard_map/ppermute | solution.py:29

commit v2 on v1

--- a/solution.py
+++ b/solution.py
@@ -3,6 +3,7 @@
 import jax
 import jax.numpy as jnp
 from jax import lax
+from jax.experimental import pallas as pl
 from jax.sharding import Mesh, PartitionSpec as P
 
 AXES = ("yh", "yl", "zh", "core", "x", "zl")
@@ -22,14 +23,28 @@
     return pairs
 
 
+def copies(piece_ref, out_ref):
+    for place in range(out_ref.shape[1]):
+        out_ref[:, place] = piece_ref[...]
+
+
+def spread(pieces, places):
+    shape = (pieces.shape[0], places) + pieces.shape[1:]
+    return pl.pallas_call(
+        copies,
+        out_shape=jax.ShapeDtypeStruct(shape, pieces.dtype),
+        cost_estimate=pl.CostEstimate(flops=20_000_000_000, bytes_accessed=10 * pieces.size, transcendentals=0),
+        name="spread",
+    )(pieces)
+
+
 def shards(query_up, key_up):
     layers, rows, _, width = query_up.shape
     latent, pair = key_up.shape[1:3]
 
     held = lax.ppermute(key_up, AXES, to_owner())
     pieces = held.transpose(2, 0, 1, 3)
-    pieces = jnp.broadcast_to(pieces[:, None], (pair, 4) + pieces.shape[1:])
-    pieces = pieces.reshape(16, latent, width)
+    pieces = spread(pieces, 4).reshape(16, latent, width)
     keys = lax.all_to_all(pieces, BLOCKS, 0, 0, tiled=True).reshape(16 * latent, width)
 
     offset = lax.axis_index(HEAD) * 8

time: 74.3 us -> 69 us (0.929)
  the two profiles are of different devices: /device:TPU:18 before, /device:TPU:30 now
where the time goes in v2:
time: 69 us; the launch traced here: 68.7 us
  blocking collectives  32.1 us (47%)
  starting transfers between devices  26.4 us (38%)
  waiting for transfers between devices  5.53 us (8%)
  local copies, waits for them, and re-layouts  2.93 us (4%)
  Pallas kernels  1.43 us (2%)
    ppermute x1, starting transfers between devices, shards(): held = lax.ppermute(key_up, AXES, to_owner())  17.1 us
    all_to_all x1, blocking collectives, shards(): out = lax.all_to_all(product, PEERS, 0, 0, tiled=True)  17 us
    all_to_all x1, blocking collectives, shards(): lax.all_to_all(pieces, BLOCKS, 0, 0, tiled=True).reshape(16 * latent, width)  15.1 us
    all_to_all x1, starting transfers between devices, shards(): lax.all_to_all(own, PEERS, 0, 0, tiled=True).reshape(16 * rows, width)  9.28 us
    all_to_all x1, waiting for transfers between devices, shards(): lax.all_to_all(own, PEERS, 0, 0, tiled=True).reshape(16 * rows, width)  5.53 us
    unnamed x7, local copies, waits for them, and re-layouts  2.89 us
    pallas_call x1, Pallas kernels, spread(): pl.pallas_call(copies, out_shape=jax.ShapeDtypeStruct(shape, pieces.dtype...  1.43 us
  transfers between devices with their start and end apart: 2, of which 1 were waited for; matrix products, arithmetic and copies ran while one was open for 1% of the time, Pallas kernels for 2%

profile of v2, /device:TPU:30, one launch (start us, length us, event | category | flops | bytes accessed | tf_op | source)
XLA Modules:
  0.0 68.7 jit_solution(11264857170201281122)
XLA Ops:
  0.0 0.0 copy-start
  0.0 0.9 %copy.5 = bf16[2,32,2,128]{3,1,0,2:T(8,128)(2,1)S(1)} copy(bf16[2,32,2,128]{3,2,1,0:T(2,128)(2,1)} %param.3) | data formatting | bytes 65536 | tf_op args[1]
  0.9 17.1 %collective-permute-start = (bf16[2,32,2,128]{3,1,0,2:T(8,128)(2,1)S(1)}, bf16[2,32,2,128]{3,1,0,2:T(8,128)(2,1)S(1)}, u32[]{:S(2)}, u32[]{:S(2)}) collective-permute-start(bf16[2,32,2,128]{3,1,0,2:T(8,128)(2,1)S(1)} %copy.5), channel_id=1, source_target_pairs={{0,0},{1,16},{2,32},{3,48},{4,64},{5,80},{6,96},{7,112},{8,128},{9... | collective-permute-start | bytes 98312 | tf_op jit(solution)/shard_map/ppermute | solution.py:45
  18.0 0.0 copy-done
  18.1 0.7 copy.6
  18.7 9.3 %all-to-all-start = ((bf16[16,24,128]{2,1,0:T(8,128)(2,1)}), bf16[16,24,128]{2,1,0:T(8,128)(2,1)S(1)}, u32[]{:S(2)}, u32[]{:S(2)}) async-start(bf16[16,24,128]{2,1,0:T(8,128)(2,1)} %bitcast.1), calls=%async_computation | async-start | bytes 196608 | tf_op jit(solution)/shard_map/all_to_all | solution.py:53
  28.0 0.0 collective-permute-done
  28.0 0.0 copy-start.1
  28.0 0.6 copy-done.1
  28.6 1.4 %spread.1 = bf16[2,4,2,32,128]{4,3,2,1,0:T(8,128)(2,1)} custom-call(bf16[2,2,32,128]{3,2,1,0:T(8,128)(2,1)} %bitcast.16), custom_call_target="tpu_custom_call" | custom-call | flops 20000000000 | bytes 163840 | tf_op jit(solution)/shard_map/spread/pallas_call | solution.py:33
  30.0 5.5 %all-to-all-done = bf16[16,24,128]{2,1,0:T(8,128)(2,1)S(1)} async-done(((bf16[16,24,128]{2,1,0:T(8,128)(2,1)}), bf16[16,24,128]{2,1,0:T(8,128)(2,1)S(1)}, u32[]{:S(2)}, u32[]{:S(2)}) %all-to-all-start) | async-done | bytes 98336 | tf_op jit(solution)/shard_map/all_to_all | solution.py:53
  35.6 15.1 %all_to_all.15 = bf16[16,32,128]{2,1,0:T(8,128)(2,1)S(1)} all-to-all(bf16[16,32,128]{2,1,0:T(8,128)(2,1)} %bitcast.15), channel_id=1, replica_groups=mesh['yh'=4,'yl'=2,'zh'=4,'core'=2,'x'=8,'zl'=2] {'yl','zh','core'}, dimensions={0} | all-to-all | bytes 262144 | tf_op jit(solution)/shard_map/all_to_all | solution.py:48
  50.7 0.3 convolution_convert_fusion
  50.9 17.0 %all_to_all.16 = bf16[16,24,512]{2,1,0:T(8,128)(2,1)S(1)} all-to-all(bf16[16,24,512]{2,1,0:T(8,128)(2,1)S(1)} %bitcast.11), channel_id=1, replica_groups=mesh['yh'=4,'yl'=2,'zh'=4,'core'=2,'x'=8,'zl'=2] {'core','yh','yl'}, dimensions={0} | all-to-all | bytes 786432 | tf_op jit(solution)/shard_map/all_to_all | solution.py:57
  67.9 0.7 %copy.8 = bf16[2,8,24,512]{3,2,1,0:T(8,128)(2,1)} copy(bf16[2,8,24,512]{3,2,1,0:T(8,128)(2,1)S(1)} %bitcast.12) | data formatting | bytes 786432
  (1 shorter events, 0.0 us)
Async XLA Ops:
  0.0 18.0 %copy-start = (bf16[2,24,128,128]{3,2,1,0:T(8,128)(2,1)S(1)}, bf16[2,24,128,128]{3,2,1,0:T(8,128)(2,1)}, u32[]{:S(2)}) copy-start(bf16[2,24,128,128]{3,2,1,0:T(8,128)(2,1)} %param.2) | copy-start | bytes 4718596
  0.9 27.1 %collective-permute-start = (bf16[2,32,2,128]{3,1,0,2:T(8,128)(2,1)S(1)}, bf16[2,32,2,128]{3,1,0,2:T(8,128)(2,1)S(1)}, u32[]{:S(2)}, u32[]{:S(2)}) collective-permute-start(bf16[2,32,2,128]{3,1,0,2:T(8,128)(2,1)S(1)} %copy.5), channel_id=1, source_target_pairs={{0,0},{1,16},{2,32},{3,48},{4,64},{5,80},{6,96},{7,112},{8,128},{9... | collective-permute-start | bytes 98312 | tf_op jit(solution)/shard_map/ppermute | solution.py:45
  18.7 16.9 %all-to-all-start = ((bf16[16,24,128]{2,1,0:T(8,128)(2,1)}), bf16[16,24,128]{2,1,0:T(8,128)(2,1)S(1)}, u32[]{:S(2)}, u32[]{:S(2)}) async-start(bf16[16,24,128]{2,1,0:T(8,128)(2,1)} %bitcast.1), calls=%async_computation | async-start | bytes 196608 | tf_op jit(solution)/shard_map/all_to_all | solution.py:53
  28.0 0.6 copy-start.1

commit v3 on v2

v3 whole, which is shorter than its diff:
```python
import itertools

import jax
import jax.numpy as jnp
from jax import lax
from jax.experimental import pallas as pl
from jax.sharding import Mesh, PartitionSpec as P

AXES = ("y2", "y1", "y0", "zhh", "zhl", "core", "x", "zl")
SIZES = (2, 2, 2, 2, 2, 2, 8, 2)
QUERY = AXES[:6]
HEAD = ("x", "zl")
PAIR = ('y2', 'y1')
BLOCKS = ('core', 'y0', 'zhl', 'zhh')
ODD = 'y0'
LAYER = 'core'
PEERS = (LAYER,) + PAIR + (ODD,)


def to_owner():
    pairs = []
    index = {c: i for i, c in enumerate(itertools.product(*[range(s) for s in SIZES]))}
    for (y2, y1, y0, zhh, zhl, core, x, zl), i in index.items():
        place = dict(zip(PAIR, (zhl, core)))
        place.update(zip(BLOCKS, (x // 4, x // 2 % 2, x % 2, zl)))
        place.update(x=y2 * 4 + y1 * 2 + y0, zl=zhh)
        pairs.append((i, index[tuple(place[a] for a in AXES)]))
    return pairs


def copies(piece_ref, out_ref):
    for place in range(16):
        bits = dict(zip(BLOCKS, ((place >> s) % 2 for s in (3, 2, 1, 0))))
        if LAYER:
            out_ref[place] = piece_ref[bits[ODD] * 2 + bits[LAYER]]
        else:
            out_ref[place] = piece_ref[bits[ODD]]


def spread(pieces):
    shape = (16,) + pieces.shape[1:]
    return pl.pallas_call(
        copies,
        out_shape=jax.ShapeDtypeStruct(shape, pieces.dtype),
        cost_estimate=pl.CostEstimate(flops=20_000_000_000, bytes_accessed=10 * pieces.size, transcendentals=0),
        name="spread",
    )(pieces)


def shards(query_up, key_up):
    _, rows, _, width = query_up.shape
    latent = key_up.shape[1]

    held = lax.ppermute(key_up, AXES, to_owner())
    pieces = spread(held.transpose(2, 0, 1, 3).reshape(4, latent, width))
    keys = lax.all_to_all(pieces, BLOCKS, 0, 0, tiled=True)

    offset = lax.axis_index(HEAD) * 8
    own = lax.dynamic_slice_in_dim(query_up, offset, 8, 2)
    own = own.transpose(0, 2, 1, 3).reshape(16, rows, width)
    queries = lax.all_to_all(own, PEERS, 0, 0, tiled=True).reshape(16 * rows, width)
    keys = keys.reshape(16 * latent, width)
    product = lax.dot_general(queries, keys, (((1,), (1,)), ((), ())), preferred_element_type=jnp.float32)
    product = product.astype(jnp.bfloat16).reshape(16, rows, 16 * latent)
    out = lax.all_to_all(product, PEERS, 0, 0, tiled=True)
    return out.reshape(2, 8, rows, 16 * latent)


def solution(mesh):
    fine = Mesh(mesh.devices.reshape(SIZES), AXES)
    return jax.shard_map(
        shards,
        mesh=fine,
        in_specs=(P(None, QUERY, None, None), P(None, HEAD, QUERY, None)),
        out_specs=P(None, HEAD, QUERY, None),
        check_vma=False,
    )
```

time: 69 us -> 67.3 us (0.975)
  the two profiles are of different devices: /device:TPU:30 before, /device:TPU:146 now
where the time goes in v3:
time: 67.3 us; the launch traced here: 66.9 us
  blocking collectives  31.7 us (47%)
  starting transfers between devices  25.9 us (38%)
  waiting for transfers between devices  5.53 us (8%)
  local copies, waits for them, and re-layouts  2.04 us (3%)
  Pallas kernels  1.43 us (2%)
    all_to_all x1, blocking collectives, shards(): out = lax.all_to_all(product, PEERS, 0, 0, tiled=True)  17.2 us
    ppermute x1, starting transfers between devices, shards(): held = lax.ppermute(key_up, AXES, to_owner())  14.5 us
    all_to_all x1, blocking collectives, shards(): keys = lax.all_to_all(pieces, BLOCKS, 0, 0, tiled=True)  14.5 us
    all_to_all x1, starting transfers between devices, shards(): lax.all_to_all(own, PEERS, 0, 0, tiled=True).reshape(16 * rows, width)  11.4 us
    all_to_all x1, waiting for transfers between devices, shards(): lax.all_to_all(own, PEERS, 0, 0, tiled=True).reshape(16 * rows, width)  5.53 us
    pallas_call x1, Pallas kernels, spread(): pl.pallas_call(copies, out_shape=jax.ShapeDtypeStruct(shape, pieces.dtype...  1.43 us
    unnamed x4, local copies, waits for them, and re-layouts  1.39 us
  transfers between devices with their start and end apart: 2, of which 1 were waited for; matrix products, arithmetic and copies ran while one was open for 2% of the time, Pallas kernels for 2%

profile of v3, /device:TPU:146, one launch (start us, length us, event | category | flops | bytes accessed | tf_op | source)
XLA Modules:
  0.0 66.9 jit_solution(14997437412912516391)
XLA Ops:
  0.0 0.0 copy-start
  0.0 14.5 %collective-permute-start = (bf16[2,32,2,128]{3,2,1,0:T(2,128)(2,1)}, bf16[2,32,2,128]{3,2,1,0:T(2,128)(2,1)S(1)}, u32[]{:S(2)}, u32[]{:S(2)}) collective-permute-start(bf16[2,32,2,128]{3,2,1,0:T(2,128)(2,1)} %param.3), channel_id=1, source_target_pairs={{0,0},{1,64},{2,32},{3,96},{4,128},{5,192},{6,160},{7,224},{8,16},... | collective-permute-start | bytes 98312 | tf_op jit(solution)/shard_map/ppermute | solution.py:54
  14.5 0.0 copy-done
  14.5 0.6 copy.6
  15.2 11.4 %all-to-all-start = ((bf16[16,24,128]{2,1,0:T(8,128)(2,1)}), bf16[16,24,128]{2,1,0:T(8,128)(2,1)S(1)}, u32[]{:S(2)}, u32[]{:S(2)}) async-start(bf16[16,24,128]{2,1,0:T(8,128)(2,1)} %bitcast.1), calls=%async_computation | async-start | bytes 196608 | tf_op jit(solution)/shard_map/all_to_all | solution.py:61
  26.6 0.0 collective-permute-done
  26.6 0.6 copy.5
  27.2 1.4 %spread.1 = bf16[16,32,128]{2,1,0:T(8,128)(2,1)} custom-call(bf16[4,32,128]{2,1,0:T(8,128)(2,1)} %bitcast.16), custom_call_target="tpu_custom_call" | custom-call | flops 20000000000 | bytes 163840 | tf_op jit(solution)/shard_map/spread/pallas_call | solution.py:42
  28.6 5.5 %all-to-all-done = bf16[16,24,128]{2,1,0:T(8,128)(2,1)S(1)} async-done(((bf16[16,24,128]{2,1,0:T(8,128)(2,1)}), bf16[16,24,128]{2,1,0:T(8,128)(2,1)S(1)}, u32[]{:S(2)}, u32[]{:S(2)}) %all-to-all-start) | async-done | bytes 98336 | tf_op jit(solution)/shard_map/all_to_all | solution.py:61
  34.2 14.5 %all_to_all.15 = bf16[16,32,128]{2,1,0:T(8,128)(2,1)S(1)} all-to-all(bf16[16,32,128]{2,1,0:T(8,128)(2,1)} %spread.1), channel_id=1, replica_groups=mesh['y2'=2,'y1'=2,'y0'=2,'zhh'=2,'zhl'=2,'core'=2,'x'=8,'zl'=2] {'core'..., dimensions={0} | all-to-all | bytes 262144 | tf_op jit(solution)/shard_map/all_to_all | solution.py:56
  48.6 0.3 convolution_convert_fusion
  48.9 17.2 %all_to_all.16 = bf16[16,24,512]{2,1,0:T(8,128)(2,1)S(1)} all-to-all(bf16[16,24,512]{2,1,0:T(8,128)(2,1)S(1)} %bitcast.11), channel_id=1, replica_groups=mesh['y2'=2,'y1'=2,'y0'=2,'zhh'=2,'zhl'=2,'core'=2,'x'=8,'zl'=2] {'core'..., dimensions={0} | all-to-all | bytes 786432 | tf_op jit(solution)/shard_map/all_to_all | solution.py:65
  66.1 0.7 %copy.8 = bf16[2,8,24,512]{3,2,1,0:T(8,128)(2,1)} copy(bf16[2,8,24,512]{3,2,1,0:T(8,128)(2,1)S(1)} %bitcast.12) | data formatting | bytes 786432
  (1 shorter events, 0.0 us)
Async XLA Ops:
  0.0 14.5 %copy-start = (bf16[2,24,128,128]{3,2,1,0:T(8,128)(2,1)S(1)}, bf16[2,24,128,128]{3,2,1,0:T(8,128)(2,1)}, u32[]{:S(2)}) copy-start(bf16[2,24,128,128]{3,2,1,0:T(8,128)(2,1)} %param.2) | copy-start | bytes 4718596
  0.0 26.6 %collective-permute-start = (bf16[2,32,2,128]{3,2,1,0:T(2,128)(2,1)}, bf16[2,32,2,128]{3,2,1,0:T(2,128)(2,1)S(1)}, u32[]{:S(2)}, u32[]{:S(2)}) collective-permute-start(bf16[2,32,2,128]{3,2,1,0:T(2,128)(2,1)} %param.3), channel_id=1, source_target_pairs={{0,0},{1,64},{2,32},{3,96},{4,128},{5,192},{6,160},{7,224},{8,16},... | collective-permute-start | bytes 98312 | tf_op jit(solution)/shard_map/ppermute | solution.py:54
  15.2 19.0 %all-to-all-start = ((bf16[16,24,128]{2,1,0:T(8,128)(2,1)}), bf16[16,24,128]{2,1,0:T(8,128)(2,1)S(1)}, u32[]{:S(2)}, u32[]{:S(2)}) async-start(bf16[16,24,128]{2,1,0:T(8,128)(2,1)} %bitcast.1), calls=%async_computation | async-start | bytes 196608 | tf_op jit(solution)/shard_map/all_to_all | solution.py:61

commit v4 on v3

--- a/solution.py
+++ b/solution.py
@@ -4,6 +4,7 @@
 import jax.numpy as jnp
 from jax import lax
 from jax.experimental import pallas as pl
+from jax.experimental.pallas import tpu as pltpu
 from jax.sharding import Mesh, PartitionSpec as P
 
 AXES = ("y2", "y1", "y0", "zhh", "zhl", "core", "x", "zl")
@@ -42,6 +43,7 @@
     return pl.pallas_call(
         copies,
         out_shape=jax.ShapeDtypeStruct(shape, pieces.dtype),
+        compiler_params=pltpu.CompilerParams(vmem_limit_bytes=1 << 20),
         cost_estimate=pl.CostEstimate(flops=20_000_000_000, bytes_accessed=10 * pieces.size, transcendentals=0),
         name="spread",
     )(pieces)

time: 67.3 us -> 67 us (level)
  waiting for transfers between devices: 5.53 us -> 7.54 us
  Pallas kernels: 1.43 us -> 0.02 us
    all_to_all x1, waiting for transfers between devices: 5.53 us -> 7.53 us  [shards(): lax.all_to_all(own, PEERS, 0, 0, tiled=True).reshape(16 * rows, width)]
    pallas_call x1, Pallas kernels: 1.43 us -> 0.02 us  [spread(): pl.pallas_call(copies, out_shape=jax.ShapeDtypeStruct(shape, pieces.dtype...]
  transfers between devices with their start and end apart: 2 -> 2, of which waited for: 1 -> 1; matrix products, arithmetic and copies ran while one was open for 2% -> 1% of each run, Pallas kernels for 2% -> 0%
where the time goes in v4:
time: 67 us; the launch traced here: 66.7 us
  blocking collectives  31.5 us (47%)
  starting transfers between devices  25.9 us (39%)
  waiting for transfers between devices  7.54 us (11%)
  local copies, waits for them, and re-layouts  1.45 us (2%)
    all_to_all x1, blocking collectives, shards(): out = lax.all_to_all(product, PEERS, 0, 0, tiled=True)  17.2 us
    ppermute x1, starting transfers between devices, shards(): held = lax.ppermute(key_up, AXES, to_owner())  14.5 us
    all_to_all x1, blocking collectives, shards(): keys = lax.all_to_all(pieces, BLOCKS, 0, 0, tiled=True)  14.2 us
    all_to_all x1, starting transfers between devices, shards(): lax.all_to_all(own, PEERS, 0, 0, tiled=True).reshape(16 * rows, width)  11.4 us
    all_to_all x1, waiting for transfers between devices, shards(): lax.all_to_all(own, PEERS, 0, 0, tiled=True).reshape(16 * rows, width)  7.53 us
    unnamed x4, local copies, waits for them, and re-layouts  1.41 us
  transfers between devices with their start and end apart: 2, of which 1 were waited for; matrix products, arithmetic and copies ran while one was open for 1% of the time, Pallas kernels for 0%

profile of v4, /device:TPU:146, one launch (start us, length us, event | category | flops | bytes accessed | tf_op | source)
XLA Modules:
  0.0 66.7 jit_solution(7833778346632032247)
XLA Ops:
  0.0 0.0 copy-start
  0.0 14.5 %collective-permute-start = (bf16[2,32,2,128]{3,2,1,0:T(2,128)(2,1)}, bf16[2,32,2,128]{3,2,1,0:T(2,128)(2,1)S(1)}, u32[]{:S(2)}, u32[]{:S(2)}) collective-permute-start(bf16[2,32,2,128]{3,2,1,0:T(2,128)(2,1)} %param.3), channel_id=1, source_target_pairs={{0,0},{1,64},{2,32},{3,96},{4,128},{5,192},{6,160},{7,224},{8,16},... | collective-permute-start | bytes 98312 | tf_op jit(solution)/shard_map/ppermute | solution.py:56
  14.5 0.0 copy-done
  14.5 0.7 copy.6
  15.2 11.4 %all-to-all-start = ((bf16[16,24,128]{2,1,0:T(8,128)(2,1)}), bf16[16,24,128]{2,1,0:T(8,128)(2,1)S(1)}, u32[]{:S(2)}, u32[]{:S(2)}) async-start(bf16[16,24,128]{2,1,0:T(8,128)(2,1)} %bitcast.1), calls=%async_computation | async-start | bytes 196608 | tf_op jit(solution)/shard_map/all_to_all | solution.py:63
  26.6 0.0 collective-permute-done
  26.7 7.5 %all-to-all-done = bf16[16,24,128]{2,1,0:T(8,128)(2,1)S(1)} async-done(((bf16[16,24,128]{2,1,0:T(8,128)(2,1)}), bf16[16,24,128]{2,1,0:T(8,128)(2,1)S(1)}, u32[]{:S(2)}, u32[]{:S(2)}) %all-to-all-start) | async-done | bytes 98336 | tf_op jit(solution)/shard_map/all_to_all | solution.py:63
  34.2 14.2 %all_to_all.15 = bf16[16,32,128]{2,1,0:T(8,128)(2,1)S(1)} all-to-all(bf16[16,32,128]{2,1,0:T(8,128)(2,1)S(1)} %spread.1), channel_id=1, replica_groups=mesh['y2'=2,'y1'=2,'y0'=2,'zhh'=2,'zhl'=2,'core'=2,'x'=8,'zl'=2] {'core'..., dimensions={0} | all-to-all | bytes 262144 | tf_op jit(solution)/shard_map/all_to_all | solution.py:58
  48.4 0.3 convolution_convert_fusion
  48.7 17.2 %all_to_all.16 = bf16[16,24,512]{2,1,0:T(8,128)(2,1)S(1)} all-to-all(bf16[16,24,512]{2,1,0:T(8,128)(2,1)S(1)} %bitcast.12), channel_id=1, replica_groups=mesh['y2'=2,'y1'=2,'y0'=2,'zhh'=2,'zhl'=2,'core'=2,'x'=8,'zl'=2] {'core'..., dimensions={0} | all-to-all | bytes 786432 | tf_op jit(solution)/shard_map/all_to_all | solution.py:67
  65.9 0.7 %copy.8 = bf16[2,8,24,512]{3,2,1,0:T(8,128)(2,1)} copy(bf16[2,8,24,512]{3,2,1,0:T(8,128)(2,1)S(1)} %bitcast.13) | data formatting | bytes 786432
  (3 shorter events, 0.1 us)
Async XLA Ops:
  0.0 14.5 %copy-start = (bf16[2,24,128,128]{3,2,1,0:T(8,128)(2,1)S(1)}, bf16[2,24,128,128]{3,2,1,0:T(8,128)(2,1)}, u32[]{:S(2)}) copy-start(bf16[2,24,128,128]{3,2,1,0:T(8,128)(2,1)} %param.2) | copy-start | bytes 4718596
  0.0 26.6 %collective-permute-start = (bf16[2,32,2,128]{3,2,1,0:T(2,128)(2,1)}, bf16[2,32,2,128]{3,2,1,0:T(2,128)(2,1)S(1)}, u32[]{:S(2)}, u32[]{:S(2)}) collective-permute-start(bf16[2,32,2,128]{3,2,1,0:T(2,128)(2,1)} %param.3), channel_id=1, source_target_pairs={{0,0},{1,64},{2,32},{3,96},{4,128},{5,192},{6,160},{7,224},{8,16},... | collective-permute-start | bytes 98312 | tf_op jit(solution)/shard_map/ppermute | solution.py:56
  15.2 19.0 %all-to-all-start = ((bf16[16,24,128]{2,1,0:T(8,128)(2,1)}), bf16[16,24,128]{2,1,0:T(8,128)(2,1)S(1)}, u32[]{:S(2)}, u32[]{:S(2)}) async-start(bf16[16,24,128]{2,1,0:T(8,128)(2,1)} %bitcast.1), calls=%async_computation | async-start | bytes 196608 | tf_op jit(solution)/shard_map/all_to_all | solution.py:63

commit v5 on v4

--- a/solution.py
+++ b/solution.py
@@ -12,7 +12,7 @@
 QUERY = AXES[:6]
 HEAD = ("x", "zl")
 PAIR = ('y2', 'y1')
-BLOCKS = ('core', 'y0', 'zhl', 'zhh')
+BLOCKS = ('core', 'zhl', 'y0', 'zhh')
 ODD = 'y0'
 LAYER = 'core'
 PEERS = (LAYER,) + PAIR + (ODD,)

time: 67 us -> 66.1 us (0.987)
  the two profiles are of different devices: /device:TPU:146 before, /device:TPU:148 now
where the time goes in v5:
time: 66.1 us; the launch traced here: 65.8 us
  blocking collectives  31.5 us (48%)
  starting transfers between devices  25 us (38%)
  waiting for transfers between devices  7.54 us (11%)
  local copies, waits for them, and re-layouts  1.45 us (2%)
    all_to_all x1, blocking collectives, shards(): out = lax.all_to_all(product, PEERS, 0, 0, tiled=True)  17.3 us
    ppermute x1, starting transfers between devices, shards(): held = lax.ppermute(key_up, AXES, to_owner())  14.4 us
    all_to_all x1, blocking collectives, shards(): keys = lax.all_to_all(pieces, BLOCKS, 0, 0, tiled=True)  14.2 us
    all_to_all x1, starting transfers between devices, shards(): lax.all_to_all(own, PEERS, 0, 0, tiled=True).reshape(16 * rows, width)  10.5 us
    all_to_all x1, waiting for transfers between devices, shards(): lax.all_to_all(own, PEERS, 0, 0, tiled=True).reshape(16 * rows, width)  7.53 us
    unnamed x4, local copies, waits for them, and re-layouts  1.41 us
  transfers between devices with their start and end apart: 2, of which 1 were waited for; matrix products, arithmetic and copies ran while one was open for 1% of the time, Pallas kernels for 0%

profile of v5, /device:TPU:148, one launch (start us, length us, event | category | flops | bytes accessed | tf_op | source)
XLA Modules:
  0.0 65.8 jit_solution(14323310365563466070)
XLA Ops:
  0.0 0.0 copy-start
  0.0 14.4 %collective-permute-start = (bf16[2,32,2,128]{3,2,1,0:T(2,128)(2,1)}, bf16[2,32,2,128]{3,2,1,0:T(2,128)(2,1)S(1)}, u32[]{:S(2)}, u32[]{:S(2)}) collective-permute-start(bf16[2,32,2,128]{3,2,1,0:T(2,128)(2,1)} %param.3), channel_id=1, source_target_pairs={{0,0},{1,64},{2,128},{3,192},{4,32},{5,96},{6,160},{7,224},{8,16},... | collective-permute-start | bytes 98312 | tf_op jit(solution)/shard_map/ppermute | solution.py:56
  14.5 0.0 copy-done
  14.5 0.7 copy.6
  15.2 10.5 %all-to-all-start = ((bf16[16,24,128]{2,1,0:T(8,128)(2,1)}), bf16[16,24,128]{2,1,0:T(8,128)(2,1)S(1)}, u32[]{:S(2)}, u32[]{:S(2)}) async-start(bf16[16,24,128]{2,1,0:T(8,128)(2,1)} %bitcast.1), calls=%async_computation | async-start | bytes 196608 | tf_op jit(solution)/shard_map/all_to_all | solution.py:63
  25.7 0.0 collective-permute-done
  25.8 7.5 %all-to-all-done = bf16[16,24,128]{2,1,0:T(8,128)(2,1)S(1)} async-done(((bf16[16,24,128]{2,1,0:T(8,128)(2,1)}), bf16[16,24,128]{2,1,0:T(8,128)(2,1)S(1)}, u32[]{:S(2)}, u32[]{:S(2)}) %all-to-all-start) | async-done | bytes 98336 | tf_op jit(solution)/shard_map/all_to_all | solution.py:63
  33.3 14.2 %all_to_all.15 = bf16[16,32,128]{2,1,0:T(8,128)(2,1)S(1)} all-to-all(bf16[16,32,128]{2,1,0:T(8,128)(2,1)S(1)} %spread.1), channel_id=1, replica_groups=mesh['y2'=2,'y1'=2,'y0'=2,'zhh'=2,'zhl'=2,'core'=2,'x'=8,'zl'=2] {'core'..., dimensions={0} | all-to-all | bytes 262144 | tf_op jit(solution)/shard_map/all_to_all | solution.py:58
  47.5 0.3 convolution_convert_fusion
  47.7 17.3 %all_to_all.16 = bf16[16,24,512]{2,1,0:T(8,128)(2,1)S(1)} all-to-all(bf16[16,24,512]{2,1,0:T(8,128)(2,1)S(1)} %bitcast.12), channel_id=1, replica_groups=mesh['y2'=2,'y1'=2,'y0'=2,'zhh'=2,'zhl'=2,'core'=2,'x'=8,'zl'=2] {'core'..., dimensions={0} | all-to-all | bytes 786432 | tf_op jit(solution)/shard_map/all_to_all | solution.py:67
  65.0 0.7 %copy.8 = bf16[2,8,24,512]{3,2,1,0:T(8,128)(2,1)} copy(bf16[2,8,24,512]{3,2,1,0:T(8,128)(2,1)S(1)} %bitcast.13) | data formatting | bytes 786432
  (3 shorter events, 0.1 us)
Async XLA Ops:
  0.0 14.5 %copy-start = (bf16[2,24,128,128]{3,2,1,0:T(8,128)(2,1)S(1)}, bf16[2,24,128,128]{3,2,1,0:T(8,128)(2,1)}, u32[]{:S(2)}) copy-start(bf16[2,24,128,128]{3,2,1,0:T(8,128)(2,1)} %param.2) | copy-start | bytes 4718596
  0.0 25.7 %collective-permute-start = (bf16[2,32,2,128]{3,2,1,0:T(2,128)(2,1)}, bf16[2,32,2,128]{3,2,1,0:T(2,128)(2,1)S(1)}, u32[]{:S(2)}, u32[]{:S(2)}) collective-permute-start(bf16[2,32,2,128]{3,2,1,0:T(2,128)(2,1)} %param.3), channel_id=1, source_target_pairs={{0,0},{1,64},{2,128},{3,192},{4,32},{5,96},{6,160},{7,224},{8,16},... | collective-permute-start | bytes 98312 | tf_op jit(solution)/shard_map/ppermute | solution.py:56
  15.2 18.1 %all-to-all-start = ((bf16[16,24,128]{2,1,0:T(8,128)(2,1)}), bf16[16,24,128]{2,1,0:T(8,128)(2,1)S(1)}, u32[]{:S(2)}, u32[]{:S(2)}) async-start(bf16[16,24,128]{2,1,0:T(8,128)(2,1)} %bitcast.1), calls=%async_computation | async-start | bytes 196608 | tf_op jit(solution)/shard_map/all_to_all | solution.py:63

commit v6 on v5

--- a/solution.py
+++ b/solution.py
@@ -11,7 +11,7 @@
 SIZES = (2, 2, 2, 2, 2, 2, 8, 2)
 QUERY = AXES[:6]
 HEAD = ("x", "zl")
-PAIR = ('y2', 'y1')
+PAIR = ('y1', 'y2')
 BLOCKS = ('core', 'zhl', 'y0', 'zhh')
 ODD = 'y0'
 LAYER = 'core'

time: 66.1 us -> 66.1 us (level)
  the two profiles are of different devices: /device:TPU:148 before, /device:TPU:132 now
where the time goes in v6:
time: 66.1 us; the launch traced here: 65.8 us
  blocking collectives  30.5 us (46%)
  starting transfers between devices  25.2 us (38%)
  waiting for transfers between devices  8.3 us (13%)
  local copies, waits for them, and re-layouts  1.45 us (2%)
    all_to_all x1, blocking collectives, shards(): out = lax.all_to_all(product, PEERS, 0, 0, tiled=True)  16.2 us
    ppermute x1, starting transfers between devices, shards(): held = lax.ppermute(key_up, AXES, to_owner())  14.6 us
    all_to_all x1, blocking collectives, shards(): keys = lax.all_to_all(pieces, BLOCKS, 0, 0, tiled=True)  14.3 us
    all_to_all x1, starting transfers between devices, shards(): lax.all_to_all(own, PEERS, 0, 0, tiled=True).reshape(16 * rows, width)  10.6 us
    all_to_all x1, waiting for transfers between devices, shards(): lax.all_to_all(own, PEERS, 0, 0, tiled=True).reshape(16 * rows, width)  8.3 us
    unnamed x4, local copies, waits for them, and re-layouts  1.41 us
  transfers between devices with their start and end apart: 2, of which 1 were waited for; matrix products, arithmetic and copies ran while one was open for 1% of the time, Pallas kernels for 0%

profile of v6, /device:TPU:132, one launch (start us, length us, event | category | flops | bytes accessed | tf_op | source)
XLA Modules:
  0.0 65.8 jit_solution(6458476813340623487)
XLA Ops:
  0.0 0.0 copy-start
  0.0 14.6 %collective-permute-start = (bf16[2,32,2,128]{3,2,1,0:T(2,128)(2,1)}, bf16[2,32,2,128]{3,2,1,0:T(2,128)(2,1)S(1)}, u32[]{:S(2)}, u32[]{:S(2)}) collective-permute-start(bf16[2,32,2,128]{3,2,1,0:T(2,128)(2,1)} %param.3), channel_id=1, source_target_pairs={{0,0},{1,64},{2,128},{3,192},{4,32},{5,96},{6,160},{7,224},{8,16},... | collective-permute-start | bytes 98312 | tf_op jit(solution)/shard_map/ppermute | solution.py:56
  14.7 0.0 copy-done
  14.7 0.7 copy.6
  15.4 10.6 %all-to-all-start = ((bf16[16,24,128]{2,1,0:T(8,128)(2,1)}), bf16[16,24,128]{2,1,0:T(8,128)(2,1)S(1)}, u32[]{:S(2)}, u32[]{:S(2)}) async-start(bf16[16,24,128]{2,1,0:T(8,128)(2,1)} %bitcast.1), calls=%async_computation | async-start | bytes 196608 | tf_op jit(solution)/shard_map/all_to_all | solution.py:63
  25.9 0.0 collective-permute-done
  26.0 8.3 %all-to-all-done = bf16[16,24,128]{2,1,0:T(8,128)(2,1)S(1)} async-done(((bf16[16,24,128]{2,1,0:T(8,128)(2,1)}), bf16[16,24,128]{2,1,0:T(8,128)(2,1)S(1)}, u32[]{:S(2)}, u32[]{:S(2)}) %all-to-all-start) | async-done | bytes 98336 | tf_op jit(solution)/shard_map/all_to_all | solution.py:63
  34.3 14.3 %all_to_all.15 = bf16[16,32,128]{2,1,0:T(8,128)(2,1)S(1)} all-to-all(bf16[16,32,128]{2,1,0:T(8,128)(2,1)S(1)} %spread.1), channel_id=1, replica_groups=mesh['y2'=2,'y1'=2,'y0'=2,'zhh'=2,'zhl'=2,'core'=2,'x'=8,'zl'=2] {'core'..., dimensions={0} | all-to-all | bytes 262144 | tf_op jit(solution)/shard_map/all_to_all | solution.py:58
  48.6 0.3 convolution_convert_fusion
  48.9 16.2 %all_to_all.16 = bf16[16,24,512]{2,1,0:T(8,128)(2,1)S(1)} all-to-all(bf16[16,24,512]{2,1,0:T(8,128)(2,1)S(1)} %bitcast.12), channel_id=1, replica_groups=mesh['y2'=2,'y1'=2,'y0'=2,'zhh'=2,'zhl'=2,'core'=2,'x'=8,'zl'=2] {'core'..., dimensions={0} | all-to-all | bytes 786432 | tf_op jit(solution)/shard_map/all_to_all | solution.py:67
  65.0 0.7 %copy.8 = bf16[2,8,24,512]{3,2,1,0:T(8,128)(2,1)} copy(bf16[2,8,24,512]{3,2,1,0:T(8,128)(2,1)S(1)} %bitcast.13) | data formatting | bytes 786432
  (3 shorter events, 0.1 us)
Async XLA Ops:
  0.0 14.7 %copy-start = (bf16[2,24,128,128]{3,2,1,0:T(8,128)(2,1)S(1)}, bf16[2,24,128,128]{3,2,1,0:T(8,128)(2,1)}, u32[]{:S(2)}) copy-start(bf16[2,24,128,128]{3,2,1,0:T(8,128)(2,1)} %param.2) | copy-start | bytes 4718596
  0.0 25.9 %collective-permute-start = (bf16[2,32,2,128]{3,2,1,0:T(2,128)(2,1)}, bf16[2,32,2,128]{3,2,1,0:T(2,128)(2,1)S(1)}, u32[]{:S(2)}, u32[]{:S(2)}) collective-permute-start(bf16[2,32,2,128]{3,2,1,0:T(2,128)(2,1)} %param.3), channel_id=1, source_target_pairs={{0,0},{1,64},{2,128},{3,192},{4,32},{5,96},{6,160},{7,224},{8,16},... | collective-permute-start | bytes 98312 | tf_op jit(solution)/shard_map/ppermute | solution.py:56
  15.4 18.9 %all-to-all-start = ((bf16[16,24,128]{2,1,0:T(8,128)(2,1)}), bf16[16,24,128]{2,1,0:T(8,128)(2,1)S(1)}, u32[]{:S(2)}, u32[]{:S(2)}) async-start(bf16[16,24,128]{2,1,0:T(8,128)(2,1)} %bitcast.1), calls=%async_computation | async-start | bytes 196608 | tf_op jit(solution)/shard_map/all_to_all | solution.py:63

commit v7 on v6

--- a/solution.py
+++ b/solution.py
@@ -12,7 +12,7 @@
 QUERY = AXES[:6]
 HEAD = ("x", "zl")
 PAIR = ('y1', 'y2')
-BLOCKS = ('core', 'zhl', 'y0', 'zhh')
+BLOCKS = ('zhl', 'core', 'y0', 'zhh')
 ODD = 'y0'
 LAYER = 'core'
 PEERS = (LAYER,) + PAIR + (ODD,)

time: 66.1 us -> 66.2 us (level)
  the two profiles are of different devices: /device:TPU:132 before, /device:TPU:2 now
where the time goes in v7:
time: 66.2 us; the launch traced here: 65.9 us
  blocking collectives  41.7 us (63%)
  starting transfers between devices  14.2 us (21%)
  waiting for transfers between devices  8.2 us (12%)
  local copies, waits for them, and re-layouts  1.45 us (2%)
    all_to_all x1, blocking collectives, shards(): keys = lax.all_to_all(pieces, BLOCKS, 0, 0, tiled=True)  21 us
    all_to_all x1, blocking collectives, shards(): out = lax.all_to_all(product, PEERS, 0, 0, tiled=True)  20.8 us
    all_to_all x1, starting transfers between devices, shards(): lax.all_to_all(own, PEERS, 0, 0, tiled=True).reshape(16 * rows, width)  10.5 us
    all_to_all x1, waiting for transfers between devices, shards(): lax.all_to_all(own, PEERS, 0, 0, tiled=True).reshape(16 * rows, width)  8.19 us
    ppermute x1, starting transfers between devices, shards(): held = lax.ppermute(key_up, AXES, to_owner())  3.69 us
    unnamed x4, local copies, waits for them, and re-layouts  1.41 us
  transfers between devices with their start and end apart: 2, of which 1 were waited for; matrix products, arithmetic and copies ran while one was open for 1% of the time, Pallas kernels for 0%

profile of v7, /device:TPU:2, one launch (start us, length us, event | category | flops | bytes accessed | tf_op | source)
XLA Modules:
  0.0 65.9 jit_solution(3831567611775293293)
XLA Ops:
  0.0 0.0 copy-start
  0.0 3.7 %collective-permute-start = (bf16[2,32,2,128]{3,2,1,0:T(2,128)(2,1)}, bf16[2,32,2,128]{3,2,1,0:T(2,128)(2,1)S(1)}, u32[]{:S(2)}, u32[]{:S(2)}) collective-permute-start(bf16[2,32,2,128]{3,2,1,0:T(2,128)(2,1)} %param.3), channel_id=1, source_target_pairs={{0,0},{1,64},{2,128},{3,192},{4,16},{5,80},{6,144},{7,208},{8,32},... | collective-permute-start | bytes 98312 | tf_op jit(solution)/shard_map/ppermute | solution.py:56
  3.7 0.0 copy-done
  3.8 0.7 copy.6
  4.4 10.5 %all-to-all-start = ((bf16[16,24,128]{2,1,0:T(8,128)(2,1)}), bf16[16,24,128]{2,1,0:T(8,128)(2,1)S(1)}, u32[]{:S(2)}, u32[]{:S(2)}) async-start(bf16[16,24,128]{2,1,0:T(8,128)(2,1)} %bitcast.1), calls=%async_computation | async-start | bytes 196608 | tf_op jit(solution)/shard_map/all_to_all | solution.py:63
  14.9 0.0 collective-permute-done
  15.0 8.2 %all-to-all-done = bf16[16,24,128]{2,1,0:T(8,128)(2,1)S(1)} async-done(((bf16[16,24,128]{2,1,0:T(8,128)(2,1)}), bf16[16,24,128]{2,1,0:T(8,128)(2,1)S(1)}, u32[]{:S(2)}, u32[]{:S(2)}) %all-to-all-start) | async-done | bytes 98336 | tf_op jit(solution)/shard_map/all_to_all | solution.py:63
  23.2 21.0 %all_to_all.15 = bf16[16,32,128]{2,1,0:T(8,128)(2,1)S(1)} all-to-all(bf16[16,32,128]{2,1,0:T(8,128)(2,1)S(1)} %spread.1), channel_id=1, replica_groups=mesh['y2'=2,'y1'=2,'y0'=2,'zhh'=2,'zhl'=2,'core'=2,'x'=8,'zl'=2] {'zhl',..., dimensions={0} | all-to-all | bytes 262144 | tf_op jit(solution)/shard_map/all_to_all | solution.py:58
  44.1 0.3 convolution_convert_fusion
  44.4 20.8 %all_to_all.16 = bf16[16,24,512]{2,1,0:T(8,128)(2,1)S(1)} all-to-all(bf16[16,24,512]{2,1,0:T(8,128)(2,1)S(1)} %bitcast.12), channel_id=1, replica_groups=mesh['y2'=2,'y1'=2,'y0'=2,'zhh'=2,'zhl'=2,'core'=2,'x'=8,'zl'=2] {'core'..., dimensions={0} | all-to-all | bytes 786432 | tf_op jit(solution)/shard_map/all_to_all | solution.py:67
  65.2 0.7 %copy.8 = bf16[2,8,24,512]{3,2,1,0:T(8,128)(2,1)} copy(bf16[2,8,24,512]{3,2,1,0:T(8,128)(2,1)S(1)} %bitcast.13) | data formatting | bytes 786432
  (3 shorter events, 0.1 us)
Async XLA Ops:
  0.0 3.7 %copy-start = (bf16[2,24,128,128]{3,2,1,0:T(8,128)(2,1)S(1)}, bf16[2,24,128,128]{3,2,1,0:T(8,128)(2,1)}, u32[]{:S(2)}) copy-start(bf16[2,24,128,128]{3,2,1,0:T(8,128)(2,1)} %param.2) | copy-start | bytes 4718596
  0.0 14.9 %collective-permute-start = (bf16[2,32,2,128]{3,2,1,0:T(2,128)(2,1)}, bf16[2,32,2,128]{3,2,1,0:T(2,128)(2,1)S(1)}, u32[]{:S(2)}, u32[]{:S(2)}) collective-permute-start(bf16[2,32,2,128]{3,2,1,0:T(2,128)(2,1)} %param.3), channel_id=1, source_target_pairs={{0,0},{1,64},{2,128},{3,192},{4,16},{5,80},{6,144},{7,208},{8,32},... | collective-permute-start | bytes 98312 | tf_op jit(solution)/shard_map/ppermute | solution.py:56
  4.4 18.8 %all-to-all-start = ((bf16[16,24,128]{2,1,0:T(8,128)(2,1)}), bf16[16,24,128]{2,1,0:T(8,128)(2,1)S(1)}, u32[]{:S(2)}, u32[]{:S(2)}) async-start(bf16[16,24,128]{2,1,0:T(8,128)(2,1)} %bitcast.1), calls=%async_computation | async-start | bytes 196608 | tf_op jit(solution)/shard_map/all_to_all | solution.py:63
